TPU v7x, 256 devices: a whole 4x4x8 slice. The times are simulated.
256 devices in a mesh: dp: 32 (over y, x, core), mp: 8 (over z).
Axes of the slice: x: 4, y: 4, z: 8, core: 2. Of those that a mesh axis runs over, the one named last changes fastest.
Arguments:
- tile_features: bfloat16 [6144, 1536], P('dp'), may hold values from -6 to 6
- tile_slide: int32 [6144, 1], P('dp'), may hold values from 0 to 31; in each aligned block of 192 rows (0 to 191, 192 to 383, ...) at most 12 rows name the same one
- slide_pair: int32 [32], replicated, may hold values from 0 to 31, each once
- reports: bfloat16 [32, 1536], P('dp'), may hold values from -6 to 6
- w_one: bfloat16 [1536, 6144], P(None, 'mp'), may hold values from -0.15625 to 0.15625
- w_two: bfloat16 [6144, 1536], P('mp'), may hold values from -0.078125 to 0.078125
- w_query: bfloat16 [1536, 1536], P(None, 'mp'), may hold values from -0.15625 to 0.15625
- w_key: bfloat16 [1536, 1536], P(None, 'mp'), may hold values from -0.15625 to 0.15625
- w_value: bfloat16 [1536, 1536], P(None, 'mp'), may hold values from -0.15625 to 0.15625
- w_out: bfloat16 [1536, 1536], P('mp'), may hold values from -0.15625 to 0.15625
Outputs:
- contrast_loss: float32 [], replicated
- grad_one: float32 [1536, 6144], P('dp', 'mp')
- grad_two: float32 [6144, 1536], P('mp', 'dp')
- grad_query: float32 [1536, 1536], P('dp', 'mp')
- grad_key: float32 [1536, 1536], P('dp', 'mp')
- grad_value: float32 [1536, 1536], P('dp', 'mp')
- grad_out: float32 [1536, 1536], P('mp', 'dp')
Inputs may be any that keep to these rules, and one draw needn't show every extreme that they name: `tile_slide`: within the 192 tiles of one device (aligned blocks) no slide has more than 12 tiles, and some slide has exactly 12; every slide has at least one tile. `slide_pair`: each report is paired with exactly one slide.
All inputs are finite; a program needn't handle non-finite values.
Results may differ from a plain program's by a relative error of at most 0.039.
Values may be sent and summed in bfloat16 or wider, within the bound.
No kernel may reach another device: no remote copies, remote signals or barrier semaphores. Data moves between devices by JAX's collectives and lax.ppermute only.
A program may use at most 128 MiB of HBM per device.

v0:
```python
import jax
import jax.numpy as jnp
from jax import lax
from jax.sharding import PartitionSpec as P

HEAD = 96


eps = 1e-05
contrast_divisor_factor = 0.07
score_scale = 10.0
loss_scale = 4096.0
finest_arithmetic_mode = lax.Precision.HIGHEST


def norm_parts(values):
    centred = values - jnp.mean(values, -1, keepdims=True)
    inverse = lax.rsqrt(jnp.mean(centred * centred, -1, keepdims=True) + eps)
    return (centred * inverse, inverse)


def gelu_value(values):
    return 0.5 * values * (1.0 + jax.scipy.special.erf(values * 0.7071067811865476))


def gelu_slope(values):
    return (
        0.5 * (1.0 + jax.scipy.special.erf(values * 0.7071067811865476))
        + values * jnp.exp(-0.5 * values * values) * 0.3989422804014327
    )


def unit_heads(values):
    return values * lax.rsqrt(jnp.mean(values * values, -1, keepdims=True) + eps)


def attend(query, keys, values, validity):
    length = query.shape[0]
    heads = query.shape[1] // HEAD
    query_unit = unit_heads(query.reshape(length, heads, HEAD))
    key_unit = unit_heads(keys.reshape(length, heads, HEAD))
    scores = jnp.einsum("qhd,khd->hqk", query_unit, key_unit, precision=finest_arithmetic_mode) * (
        score_scale / HEAD
    )
    weights = jnp.exp(scores) * validity[None, None, :]
    weights = weights / jnp.sum(weights, -1, keepdims=True)
    mixed = jnp.einsum(
        "hqk,khd->qhd",
        weights,
        values.reshape(length, heads, HEAD),
        precision=finest_arithmetic_mode,
    )
    return mixed.reshape(length, heads * HEAD)


def contrast_all(pooled, report_float, slide_pair):
    inverse = lax.rsqrt(jnp.sum(pooled * pooled, -1, keepdims=True) + eps)
    unit_mean_image_vector = pooled * inverse
    unit_caption_vector = report_float * lax.rsqrt(
        jnp.sum(report_float * report_float, -1, keepdims=True) + eps
    )
    affinity_matrix_entries = (
        jnp.dot(unit_mean_image_vector, unit_caption_vector.T, precision=finest_arithmetic_mode)
        / contrast_divisor_factor
    )
    expo = jnp.exp(affinity_matrix_entries)
    row_total = jnp.sum(expo, 1)
    column_total = jnp.sum(expo, 0)
    count_all = affinity_matrix_entries.shape[0]
    target = (slide_pair[:, None] == jnp.arange(count_all, dtype=jnp.int32)[None, :]).astype(
        jnp.float32
    )
    positive = jnp.sum(affinity_matrix_entries * target, 1)
    loss_value = (
        jnp.sum(-positive + 0.5 * jnp.log(row_total)) + 0.5 * jnp.sum(jnp.log(column_total))
    ) / count_all
    affinity_matrix_derivative = (
        0.5 * expo / row_total[:, None] + 0.5 * expo / column_total[None, :] - target
    ) * (loss_scale / count_all)
    unit_mean_image_derivative = (
        jnp.dot(affinity_matrix_derivative, unit_caption_vector, precision=finest_arithmetic_mode)
        / contrast_divisor_factor
    )
    grad_pooled = (
        unit_mean_image_derivative
        - unit_mean_image_vector
        * jnp.sum(unit_mean_image_vector * unit_mean_image_derivative, -1, keepdims=True)
    ) * inverse
    return (loss_value, grad_pooled)


def per_device(
    tile_features, tile_slide, slide_pair, reports, w_one, w_two, w_query, w_key, w_value, w_out
):
    owners = lax.axis_size("dp")
    tile_count = tile_features.shape[0]
    width = tile_features.shape[1]
    capacity = 2 * tile_count // owners
    owner_index = lax.axis_index("dp")
    tile_float = tile_features.astype(jnp.float32)
    tile_normed, unused = norm_parts(tile_float)
    tile_norm = tile_normed.astype(jnp.bfloat16)
    hidden_pre = jnp.dot(tile_norm, w_one, preferred_element_type=jnp.float32)
    hidden = gelu_value(hidden_pre).astype(jnp.bfloat16)
    partial_out = jnp.dot(hidden, w_two, preferred_element_type=jnp.float32)
    embedding = (tile_float + lax.psum(partial_out, "mp")).astype(jnp.bfloat16)
    slide_ids = tile_slide[:, 0]
    matches = (slide_ids[:, None] == jnp.arange(owners, dtype=jnp.int32)[None, :]).astype(jnp.int32)
    ordinal = jnp.sum(matches * (jnp.cumsum(matches, 0) - 1), 1)
    position = slide_ids * capacity + ordinal
    dispatch = (
        jnp.arange(owners * capacity, dtype=jnp.int32)[:, None] == position[None, :]
    ).astype(jnp.bfloat16)
    outgoing = jnp.dot(dispatch, embedding, preferred_element_type=jnp.float32).astype(jnp.bfloat16)
    outgoing = outgoing.reshape(owners, capacity, embedding.shape[1])
    occupied = (
        jnp.sum(dispatch.astype(jnp.float32), 1).astype(jnp.bfloat16).reshape(owners, capacity)
    )
    arrived, present = (
        lax.all_to_all(outgoing, "dp", split_axis=0, concat_axis=0, tiled=True),
        lax.all_to_all(occupied, "dp", split_axis=0, concat_axis=0, tiled=True),
    )
    length = owners * capacity
    slide_rows = arrived.reshape(length, width)
    validity = present.reshape(length).astype(jnp.float32)
    rows_float = slide_rows.astype(jnp.float32)
    normed, inverse = norm_parts(rows_float)
    slide_norm = normed.astype(jnp.bfloat16)
    query = jnp.dot(slide_norm, w_query, preferred_element_type=jnp.float32)
    keys = jnp.dot(slide_norm, w_key, preferred_element_type=jnp.float32)
    values = jnp.dot(slide_norm, w_value, preferred_element_type=jnp.float32)
    attended = attend(query, keys, values, validity).astype(jnp.bfloat16)
    head_part = jnp.dot(attended, w_out, preferred_element_type=jnp.float32)
    output = rows_float + lax.psum(head_part.astype(jnp.bfloat16), "mp").astype(jnp.float32)
    tile_total = jnp.sum(validity)
    pooled = jnp.sum(output * validity[:, None], 0) / tile_total
    all_reports = lax.all_gather(reports, "dp", axis=0, tiled=True).astype(jnp.float32)
    all_pooled = lax.all_gather(pooled[None, :], "dp", axis=0, tiled=True)
    contrast_loss, grad_all = contrast_all(all_pooled, all_reports, slide_pair)
    grad_pooled = lax.dynamic_slice_in_dim(grad_all, owner_index, 1, 0)[0]
    grad_rows_out = validity[:, None] * grad_pooled[None, :] / tile_total
    grad_low = grad_rows_out.astype(jnp.bfloat16)
    grad_wo = jnp.dot(attended.T, grad_low, preferred_element_type=jnp.float32)
    grad_attended = jnp.dot(grad_low, w_out.T, preferred_element_type=jnp.float32)
    unused_out, pull = jax.vjp(lambda qa, ka, va: attend(qa, ka, va, validity), query, keys, values)
    grad_q, grad_k, grad_v = pull(grad_attended)
    grad_q = grad_q.astype(jnp.bfloat16)
    grad_k = grad_k.astype(jnp.bfloat16)
    grad_v = grad_v.astype(jnp.bfloat16)
    grad_wq = jnp.dot(slide_norm.T, grad_q, preferred_element_type=jnp.float32)
    grad_wk = jnp.dot(slide_norm.T, grad_k, preferred_element_type=jnp.float32)
    grad_wv = jnp.dot(slide_norm.T, grad_v, preferred_element_type=jnp.float32)
    grad_normed = jnp.dot(grad_q, w_query.T, preferred_element_type=jnp.float32)
    grad_normed = grad_normed + jnp.dot(grad_k, w_key.T, preferred_element_type=jnp.float32)
    grad_normed = grad_normed + jnp.dot(grad_v, w_value.T, preferred_element_type=jnp.float32)
    grad_query, grad_key, grad_value, grad_out = (
        lax.psum_scatter(
            grad_wq.astype(jnp.bfloat16), "dp", scatter_dimension=0, tiled=True
        ).astype(jnp.float32),
        lax.psum_scatter(
            grad_wk.astype(jnp.bfloat16), "dp", scatter_dimension=0, tiled=True
        ).astype(jnp.float32),
        lax.psum_scatter(
            grad_wv.astype(jnp.bfloat16), "dp", scatter_dimension=0, tiled=True
        ).astype(jnp.float32),
        lax.psum_scatter(
            grad_wo.astype(jnp.bfloat16), "dp", scatter_dimension=1, tiled=True
        ).astype(jnp.float32),
    )
    normed_total = lax.psum(grad_normed.astype(jnp.bfloat16), "mp").astype(jnp.float32)
    first = jnp.mean(normed_total, -1, keepdims=True)
    second = jnp.mean(normed_total * normed, -1, keepdims=True)
    grad_rows = grad_rows_out + (normed_total - first - normed * second) * inverse
    row_cols = grad_rows.shape[1]
    sending = grad_rows.astype(jnp.bfloat16).reshape(owners, capacity, row_cols)
    returned = lax.all_to_all(sending, "dp", split_axis=0, concat_axis=0, tiled=True)
    grad_embedding = jnp.take(returned.reshape(owners * capacity, row_cols), position, axis=0)
    grad_two_local = jnp.dot(hidden.T, grad_embedding, preferred_element_type=jnp.float32)
    grad_hidden = (
        jnp.dot(grad_embedding, w_two.T, preferred_element_type=jnp.float32)
        * gelu_slope(hidden_pre)
    ).astype(jnp.bfloat16)
    grad_one_local = jnp.dot(tile_norm.T, grad_hidden, preferred_element_type=jnp.float32)
    grad_one, grad_two = (
        lax.psum_scatter(
            grad_one_local.astype(jnp.bfloat16), "dp", scatter_dimension=0, tiled=True
        ).astype(jnp.float32),
        lax.psum_scatter(
            grad_two_local.astype(jnp.bfloat16), "dp", scatter_dimension=1, tiled=True
        ).astype(jnp.float32),
    )
    return (contrast_loss, grad_one, grad_two, grad_query, grad_key, grad_value, grad_out)


def solution(mesh):
    return jax.shard_map(
        per_device,
        mesh=mesh,
        in_specs=(
            P("dp", None),
            P("dp", None),
            P(),
            P("dp", None),
            P(None, "mp"),
            P("mp", None),
            P(None, "mp"),
            P(None, "mp"),
            P(None, "mp"),
            P("mp", None),
        ),
        out_specs=(
            P(),
            P("dp", "mp"),
            P("mp", "dp"),
            P("dp", "mp"),
            P("dp", "mp"),
            P("dp", "mp"),
            P("mp", "dp"),
        ),
        check_vma=False,
    )
```

profile of v0, /device:TPU:8, one launch (start us, length us, event | category | flops | bytes accessed | tf_op | source)
XLA Modules:
  0.0 878.7 jit_solution(226750614923202406)
XLA Ops:
  7.2 1.4 convert_reduce_fusion.2
  8.7 1.4 fusion.11
  10.1 2.3 fusion.74
  13.3 1.7 fusion.76
  17.5 7.5 all-to-all-start.1
  25.0 69.5 %all-reduce.5.cloned.1.call-done = f32[192,1536]{1,0:T(8,128)} async-done(((f32[192,1536]{1,0:T(8,128)}), f32[192,1536]{1,0:T(8,128)}) %all-reduce.5.cloned.1.call-update) | async-done | bytes 1179664 | tf_op jit(solution)/shard_map/psum | solution.py:106
  94.6 2.9 convolution_convert_fusion.3
  97.4 3.0 reshape.282
  100.4 7.5 all-to-all-start
  109.3 19.9 %all-to-all-done = bf16[32,12,1536]{2,1,0:T(8,128)(2,1)} async-done(((bf16[32,12,1536]{2,1,0:T(8,128)(2,1)}), bf16[32,12,1536]{2,1,0:T(8,128)(2,1)}, u32[]{:S(2)}, u32[]{:S(2)}) %all-to-all-start) | async-done | bytes 1179680 | tf_op jit(solution)/shard_map/all_to_all | solution.py:120
  129.2 1.7 convert_reduce_fusion.1
  131.0 2.0 multiply_reduce_fusion
  133.6 3.0 multiply_convert_fusion
  136.6 2.2 reshape.304
  138.9 1.7 fusion.77
  146.1 1.5 convolution_convert_fusion.2
  147.7 24.5 %all-gather.2 = bf16[32,1,1536]{2,1,0:T(2,128)(2,1)S(1)} all-gather(bf16[1,1,1536]{2,1,0:T(2,128)(2,1)} %bitcast.105), channel_id=1, replica_groups=mesh['dp'=32,'mp'=8] {'dp'}, dimensions={0}, use_global_device_ids=true | all-gather | bytes 101376 | tf_op jit(solution)/shard_map/all_gather | solution.py:137
  174.7 3.1 reshape.287
  179.0 41.8 %all-reduce.7.cloned.1.call-done = bf16[384,1536]{1,0:T(8,128)(2,1)} async-done(((bf16[384,1536]{1,0:T(8,128)(2,1)}), bf16[384,1536]{1,0:T(8,128)(2,1)}) %all-reduce.7.cloned.1.call-update) | async-done | bytes 1179664 | tf_op jit(solution)/shard_map/psum | solution.py:134
  220.8 2.4 multiply_reduce_fusion.1
  224.0 24.6 %all-gather.1 = f32[32,1,1536]{2,1,0:T(1,128)S(1)} all-gather(f32[1,1,1536]{2,1,0:T(1,128)S(1)} %reshape.298), channel_id=2, replica_groups=mesh['dp'=32,'mp'=8] {'dp'}, dimensions={0}, use_global_device_ids=true | all-gather | bytes 202752 | tf_op jit(solution)/shard_map/all_gather | solution.py:138
  254.1 1.4 convolution_convert_fusion.8
  262.6 1.6 fusion
  265.1 2.3 convolution_convert_fusion.4
  267.5 2.2 convert_element_type.173
  269.7 2.5 convolution_convert_fusion.6
  273.2 1.4 rsqrt.64
  274.6 2.4 convolution_convert_fusion.7
  277.0 60.4 %all-reduce.9.cloned.1.call-done = bf16[384,1536]{1,0:T(8,128)(2,1)} async-done(((bf16[384,1536]{1,0:T(8,128)(2,1)}), bf16[384,1536]{1,0:T(8,128)(2,1)}) %all-reduce.9.cloned.1.call-update) | async-done | bytes 1179664 | tf_op jit(solution)/shard_map/psum | solution.py:170
  337.4 3.0 convert_reduce_fusion
  340.5 2.6 fusion.4
  343.2 3.0 reshape.284
  346.1 7.5 all-to-all-start.2
  353.7 2.4 convolution_convert_fusion.5
  356.2 18.7 %all-to-all-done.2 = bf16[32,12,1536]{2,1,0:T(8,128)(2,1)} async-done(((bf16[32,12,1536]{2,1,0:T(8,128)(2,1)}), bf16[32,12,1536]{2,1,0:T(8,128)(2,1)}, u32[]{:S(2)}, u32[]{:S(2)}) %all-to-all-start.2) | async-done | bytes 1179680 | tf_op jit(solution)/shard_map/all_to_all | solution.py:176
  374.9 2.2 reshape.285
  377.2 1.9 gather_fusion
  379.1 4.6 convolution_convert_fusion.1
  384.9 2.3 convolution_convert_fusion
  390.4 33.8 %reduce-scatter.17.cloned.1.call-done = bf16[192,48]{0,1:T(8,128)(2,1)} async-done(((bf16[192,1536]{0,1:T(8,128)(2,1)}), bf16[192,48]{0,1:T(8,128)(2,1)}) %reduce-scatter.17.cloned.1.call-update) | async-done | bytes 18448 | tf_op jit(solution)/shard_map/reduce_scatter | solution.py:166
  425.6 86.8 %reduce-scatter.13.cloned.1.call-done = bf16[48,192]{1,0:T(8,128)(2,1)} async-done(((bf16[1536,192]{1,0:T(8,128)(2,1)}), bf16[48,192]{1,0:T(8,128)(2,1)}) %reduce-scatter.13.cloned.1.call-update) | async-done | bytes 18448 | tf_op jit(solution)/shard_map/reduce_scatter | solution.py:160
  513.7 86.8 %reduce-scatter.11.cloned.1.call-done = bf16[48,192]{1,0:T(8,128)(2,1)} async-done(((bf16[1536,192]{1,0:T(8,128)(2,1)}), bf16[48,192]{1,0:T(8,128)(2,1)}) %reduce-scatter.11.cloned.1.call-update) | async-done | bytes 18448 | tf_op jit(solution)/shard_map/reduce_scatter | solution.py:157
  600.5 1.4 convert_element_type.202
  601.8 86.9 %reduce-scatter.15.cloned.1.call-done = bf16[48,192]{1,0:T(8,128)(2,1)} async-done(((bf16[1536,192]{1,0:T(8,128)(2,1)}), bf16[48,192]{1,0:T(8,128)(2,1)}) %reduce-scatter.15.cloned.1.call-update) | async-done | bytes 18448 | tf_op jit(solution)/shard_map/reduce_scatter | solution.py:163
  690.1 88.8 %reduce-scatter.7.cloned.1.call-done = bf16[48,768]{1,0:T(8,128)(2,1)} async-done(((bf16[1536,768]{1,0:T(8,128)(2,1)}), bf16[48,768]{1,0:T(8,128)(2,1)}) %reduce-scatter.7.cloned.1.call-update) | async-done | bytes 73744 | tf_op jit(solution)/shard_map/reduce_scatter | solution.py:185
  778.9 1.6 convert_element_type.198
  780.4 89.1 %reduce-scatter.9.cloned.1.call-done = bf16[768,48]{0,1:T(8,128)(2,1)} async-done(((bf16[768,1536]{0,1:T(8,128)(2,1)}), bf16[768,48]{0,1:T(8,128)(2,1)}) %reduce-scatter.9.cloned.1.call-update) | async-done | bytes 73744 | tf_op jit(solution)/shard_map/reduce_scatter | solution.py:188
  869.5 1.6 convert_element_type.200
  (201 shorter events, 36.9 us)
Async XLA Ops:
  7.2 6.1 copy-start
  7.2 2.9 copy-start.6
  7.2 87.4 %all-reduce.5.cloned.1.call-start = ((), (), s32[]{:S(2)}) async-start(), calls=%async_computation.9 | async-start | bytes 2359296 | tf_op jit(solution)/shard_map/psum | solution.py:106
  8.7 3.8 copy-start.51
  10.0 2.4 copy-start.59
  17.5 82.9 %all-to-all-start.1 = ((bf16[32,1,12]{2,1,0:T(2,128)(2,1)}), bf16[32,1,12]{2,1,0:T(2,128)(2,1)S(1)}, u32[]{:S(2)}, u32[]{:S(2)}) async-start(bf16[32,1,12]{2,1,0:T(2,128)(2,1)} %all_to_all.16), calls=%async_computation.1 | async-start | bytes 32768 | tf_op jit(solution)/shard_map/all_to_all | solution.py:121
  100.4 28.8 %all-to-all-start = ((bf16[32,12,1536]{2,1,0:T(8,128)(2,1)}), bf16[32,12,1536]{2,1,0:T(8,128)(2,1)}, u32[]{:S(2)}, u32[]{:S(2)}) async-start(bf16[32,12,1536]{2,1,0:T(8,128)(2,1)} %reshape.282), calls=%async_computation | async-start | bytes 3145728 | tf_op jit(solution)/shard_map/all_to_all | solution.py:120
  107.9 113.0 %all-reduce.7.cloned.1.call-start = ((), (), s32[]{:S(2)}) async-start(), calls=%async_computation.10 | async-start | bytes 2359296 | tf_op jit(solution)/shard_map/psum | solution.py:134
  138.8 1.7 copy-start.9
  140.5 3.8 copy-start.19
  141.1 3.2 copy-start.4
  141.2 3.2 copy-start.38
  141.2 1.9 copy-start.27
  142.3 2.0 copy-start.40
  142.3 2.0 copy-start.31
  142.3 2.0 copy-start.33
  144.4 1.7 copy-start.22
  147.6 189.8 %all-reduce.9.cloned.1.call-start = ((), (), s32[]{:S(2)}) async-start(), calls=%async_computation.11 | async-start | bytes 2359296 | tf_op jit(solution)/shard_map/psum | solution.py:170
  220.8 28.6 %copy-start.8 = (f32[32,1,1536]{2,1,0:T(1,128)S(1)}, f32[32,1,1536]{2,1,0:T(1,128)}, u32[]{:S(2)}) copy-start(f32[32,1,1536]{2,1,0:T(1,128)} %convert_element_type.211) | copy-start | bytes 589828
  220.8 28.6 %copy-start.53 = (s32[32]{0:T(128)S(1)}, s32[32]{0:T(128)}, u32[]{:S(2)}) copy-start(s32[32]{0:T(128)} %param.12) | copy-start | bytes 388
  220.8 28.6 %copy-start.58 = (f32[32]{0:T(128)S(1)}, f32[32]{0:T(128)}, u32[]{:S(2)}) copy-start(f32[32]{0:T(128)} %add_rsqrt_fusion.2) | copy-start | bytes 388
  223.3 29.5 %copy-start.23 = (bf16[192,1536]{1,0:T(8,128)(2,1)S(1)}, bf16[192,1536]{1,0:T(8,128)(2,1)}, u32[]{:S(2)}) copy-start(bf16[192,1536]{1,0:T(8,128)(2,1)} %param.19) | copy-start | bytes 1769476
  223.3 29.5 %copy-start.28 = (f32[384]{0:T(512)S(1)}, f32[384]{0:T(512)}, u32[]{:S(2)}) copy-start(f32[384]{0:T(512)} %reshape.288) | copy-start | bytes 4612
  250.4 3.7 copy-start.54
  250.4 3.7 copy-start.56
  254.1 1.4 copy-start.20
  254.1 1.4 copy-start.48
  255.6 6.5 copy-start.21
  257.9 1.4 copy-start.32
  264.2 160.0 %reduce-scatter.17.cloned.1.call-start = ((), (), s32[]{:S(2)}) async-start(), calls=%async_computation.17 | async-start | bytes 811008 | tf_op jit(solution)/shard_map/reduce_scatter | solution.py:166
  267.4 244.9 %reduce-scatter.13.cloned.1.call-start = ((), (), s32[]{:S(2)}) async-start(), calls=%async_computation.15 | async-start | bytes 811008 | tf_op jit(solution)/shard_map/reduce_scatter | solution.py:160
  272.2 328.3 %reduce-scatter.11.cloned.1.call-start = ((), (), s32[]{:S(2)}) async-start(), calls=%async_computation.14 | async-start | bytes 811008 | tf_op jit(solution)/shard_map/reduce_scatter | solution.py:157
  274.6 62.9 %copy-start.44 = (f32[384]{0:T(512)S(1)}, f32[384]{0:T(512)}, u32[]{:S(2)}) copy-start(f32[384]{0:T(512)} %div.154) | copy-start | bytes 4612
  277.0 63.5 %copy-start.30 = (f32[384]{0:T(512)S(1)}, f32[384]{0:T(512)}, u32[]{:S(2)}) copy-start(f32[384]{0:T(512)} %reshape.288) | copy-start | bytes 4612
  277.0 63.5 %copy-start.37 = (f32[1536]{0:T(1024)S(1)}, f32[1536]{0:T(1024)}, u32[]{:S(2)}) copy-start(f32[1536]{0:T(1024)} %copy-done.35) | copy-start | bytes 18436
  337.4 3.1 copy-start.1
  337.4 3.1 copy-start.7
  337.4 3.1 copy-start.45
  346.1 28.8 %all-to-all-start.2 = ((bf16[32,12,1536]{2,1,0:T(8,128)(2,1)}), bf16[32,12,1536]{2,1,0:T(8,128)(2,1)}, u32[]{:S(2)}, u32[]{:S(2)}) async-start(bf16[32,12,1536]{2,1,0:T(8,128)(2,1)} %reshape.284), calls=%async_computation.2 | async-start | bytes 3145728 | tf_op jit(solution)/shard_map/all_to_all | solution.py:176
  353.6 2.6 copy-start.47
  353.6 2.6 copy-start.50
  353.6 335.1 %reduce-scatter.15.cloned.1.call-start = ((), (), s32[]{:S(2)}) async-start(), calls=%async_computation.16 | async-start | bytes 811008 | tf_op jit(solution)/shard_map/reduce_scatter | solution.py:163
  356.1 422.8 %reduce-scatter.7.cloned.1.call-start = ((), (), s32[]{:S(2)}) async-start(), calls=%async_computation.12 | async-start | bytes 2433024 | tf_op jit(solution)/shard_map/reduce_scatter | solution.py:185
  377.2 2.0 copy-start.52
  377.2 2.0 copy-start.60
  383.7 485.8 %reduce-scatter.9.cloned.1.call-start = ((), (), s32[]{:S(2)}) async-start(), calls=%async_computation.13 | async-start | bytes 2433024 | tf_op jit(solution)/shard_map/reduce_scatter | solution.py:188
  387.2 1.8 copy-start.55
  387.2 1.8 copy-start.61
  (26 other events, 25.0 us)
Sparse Core Ops, SparseCore 0:
  15.1 79.3 all-reduce.4
  147.8 73.0 all-reduce.6
  264.3 73.0 all-reduce.8
  341.0 83.1 reduce-scatter.16
  427.8 84.4 reduce-scatter.12
  516.0 84.4 reduce-scatter.10
  604.2 84.4 reduce-scatter.14
  692.6 86.2 reduce-scatter.6
  783.2 86.2 reduce-scatter.8
where the time goes:
time: 881 us; the launch traced here: 879 us
  waiting for transfers between devices  683 us (78%)
  blocking collectives  49.1 us (6%)
  matrix products  40.3 us (5%)
  other arithmetic  35.2 us (4%)
  local copies, waits for them, and re-layouts  31.2 us (4%)
  starting transfers between devices  23 us (3%)
  between operations  17.2 us (2%)
    reduce_scatter x1, waiting for transfers between devices, per_device(): lax.psum_scatter(grad_two_local.astype(jnp.bfloat16), 'dp', scatter_dimen...  89.1 us
    reduce_scatter x1, waiting for transfers between devices, per_device(): lax.psum_scatter(grad_one_local.astype(jnp.bfloat16), 'dp', scatter_dimen...  88.8 us
    reduce_scatter x1, waiting for transfers between devices, per_device(): lax.psum_scatter(grad_wv.astype(jnp.bfloat16), 'dp', scatter_dimension=0,...  86.9 us
    reduce_scatter x1, waiting for transfers between devices, per_device(): lax.psum_scatter(grad_wk.astype(jnp.bfloat16), 'dp', scatter_dimension=0,...  86.8 us
    reduce_scatter x1, waiting for transfers between devices, per_device(): lax.psum_scatter(grad_wq.astype(jnp.bfloat16), 'dp', scatter_dimension=0,...  86.8 us
    psum x1, waiting for transfers between devices, per_device(): embedding = (tile_float + lax.psum(partial_out, 'mp')).astype(jnp.bfloat16)  69.5 us
    psum x1, waiting for transfers between devices, per_device(): lax.psum(grad_normed.astype(jnp.bfloat16), 'mp').astype(jnp.float32)  60.4 us
    psum x1, waiting for transfers between devices, per_device(): lax.psum(head_part.astype(jnp.bfloat16), 'mp').astype(jnp.float32)  41.8 us
  transfers between devices with their start and end apart: 12, of which 11 were waited for; matrix products, arithmetic and copies ran while one was open for 6% of the time, Pallas kernels for 0%

commit v1 on v0

v1 whole, which is shorter than its diff:
```python
import jax
import jax.numpy as jnp
from jax import lax
from jax.sharding import Mesh, PartitionSpec as P

HEAD = 96
CORES = 2
ROWS = 16

eps = 1e-05
contrast_divisor_factor = 0.07
score_scale = 10.0
loss_scale = 4096.0
exact = lax.Precision.HIGHEST
f32 = jnp.float32
bf16 = jnp.bfloat16
DP = ("chip", "core")


def contract(left, right, left_dim, right_dim, **kw):
    return lax.dot_general(
        left, right, (((left_dim,), (right_dim,)), ((), ())), preferred_element_type=f32, **kw
    )


def exchange(values, axis):
    return lax.all_to_all(values, axis, 0, 0, tiled=True)


def spread(values, axis, count):
    copies = jnp.broadcast_to(values[None], (count,) + values.shape)
    return exchange(lax.optimization_barrier(copies), axis)


def gelu_value(values):
    return 0.5 * values * (1.0 + jax.scipy.special.erf(values * 0.7071067811865476))


def gelu_slope(values):
    return (
        0.5 * (1.0 + jax.scipy.special.erf(values * 0.7071067811865476))
        + values * jnp.exp(-0.5 * values * values) * 0.3989422804014327
    )


def pick(values, index, axis):
    return lax.dynamic_index_in_dim(values, index, axis, keepdims=False)


def per_device(
    tile_features, tile_slide, slide_pair, reports, w_one, w_two, w_query, w_key, w_value, w_out
):
    chips = lax.axis_size("chip")
    owners = chips * CORES
    parts = lax.axis_size("mp")
    core = lax.axis_index("core")
    owner_index = lax.axis_index(DP)
    part_index = lax.axis_index("mp")
    tiles, width = tile_features.shape
    capacity = 2 * tiles // owners
    length = owners * capacity
    block = width // parts
    share = width // owners
    heads = w_query.shape[1] // HEAD

    all_reports = spread(reports, DP, owners).reshape(owners, width).astype(f32)
    report_unit = all_reports * lax.rsqrt(
        jnp.sum(all_reports * all_reports, -1, keepdims=True) + eps
    )

    tile_float = tile_features.astype(f32)
    centred = tile_float - jnp.mean(tile_float, -1, keepdims=True)
    tile_norm = (centred * lax.rsqrt(jnp.mean(centred * centred, -1, keepdims=True) + eps)).astype(
        bf16
    )
    hidden_pre = jnp.dot(tile_norm, w_one, preferred_element_type=f32)
    hidden = gelu_value(hidden_pre).astype(bf16)
    partial_out = jnp.dot(hidden, w_two, preferred_element_type=f32).astype(bf16)
    partial_out = partial_out.reshape(tiles, parts, block).transpose(1, 0, 2)
    summed = jnp.sum(exchange(partial_out, "mp").astype(f32), 0)
    own_columns = pick(tile_features.reshape(tiles, parts, block), part_index, 1)
    embedding = (own_columns.astype(f32) + summed).astype(bf16)

    slide_ids = tile_slide[:, 0]
    matches = (slide_ids[:, None] == jnp.arange(owners, dtype=jnp.int32)[None, :]).astype(jnp.int32)
    ordinal = jnp.sum(matches * (jnp.cumsum(matches, 0) - 1), 1)
    position = slide_ids * ROWS + ordinal
    dispatch = (
        jnp.arange(owners * ROWS, dtype=jnp.int32)[:, None] == position[None, :]
    ).astype(bf16)
    flagged = jnp.concatenate(
        [embedding, jnp.ones((tiles, 1), bf16), jnp.zeros((tiles, 255 - block), bf16)], 1
    )
    outgoing = jnp.dot(dispatch, flagged, preferred_element_type=f32).astype(bf16)
    arrived = exchange(outgoing.reshape(owners, ROWS, 256), DP).reshape(owners * ROWS, 256)
    slot = jnp.arange(owners * ROWS, dtype=jnp.int32)
    row_of_slot = jnp.where(slot % ROWS < capacity, slot // ROWS * capacity + slot % ROWS, -1)
    select = (row_of_slot[:, None] == jnp.arange(length, dtype=jnp.int32)[None, :]).astype(bf16)
    chunk = contract(arrived, select, 0, 0)
    validity = chunk[block]
    valid_low = validity.astype(bf16)[None, :]
    chunk = chunk[:block].astype(bf16)
    count = jnp.sum(validity)
    slide = spread(chunk, "mp", parts).reshape(width, length)

    slide_float = slide.astype(f32)
    mean = jnp.mean(slide_float, 0, keepdims=True)
    centred = slide_float - mean
    inverse = lax.rsqrt(jnp.mean(centred * centred, 0, keepdims=True) + eps)
    normed = centred * inverse
    slide_norm = normed.astype(bf16)
    weights_in = jnp.concatenate([w_query, w_key, w_value], 1)
    projected = contract(weights_in, slide_norm, 0, 0).reshape(3, heads, HEAD, length)
    query, keys, values = projected[0], projected[1], projected[2]
    query_scale = lax.rsqrt(jnp.mean(query * query, 1, keepdims=True) + eps)
    key_scale = lax.rsqrt(jnp.mean(keys * keys, 1, keepdims=True) + eps)
    query_unit = query * query_scale
    key_unit = keys * key_scale
    query_low = query_unit.astype(bf16)
    key_low = key_unit.astype(bf16)
    scores = jnp.einsum("hdk,hdq->hkq", key_low, query_low, preferred_element_type=f32) * (
        score_scale / HEAD
    )
    weights = jnp.exp(scores) * validity[None, :, None]
    weights = weights / jnp.sum(weights, 1, keepdims=True)
    attended = jnp.einsum(
        "hdk,hkq->hdq", values.astype(bf16), weights.astype(bf16), preferred_element_type=f32
    )
    attended = attended.reshape(heads * HEAD, length).astype(bf16)
    key_mass = jnp.sum(weights * validity[None, None, :], 2)
    attended_sum = contract(valid_low, attended, 1, 1)
    slide_sum = contract(valid_low, slide, 1, 1)
    pooled_part = jnp.dot(attended_sum, w_out.astype(f32), precision=exact)
    pooled = jnp.sum(spread(pooled_part, "mp", parts), 0)
    pooled = ((pooled + slide_sum) / count)[0]

    pooled_inverse = lax.rsqrt(jnp.sum(pooled * pooled) + eps)
    pooled_unit = pooled * pooled_inverse
    logits_row = jnp.sum(report_unit * pooled_unit[None, :], -1) / contrast_divisor_factor
    logits_row = jnp.pad(logits_row, (0, 128 - owners))[None, :]
    logits = spread(logits_row, DP, owners)[:, 0, :owners]
    expo = jnp.exp(logits)
    row_total = jnp.sum(expo, 1)
    column_total = jnp.sum(expo, 0)
    target = (slide_pair[:, None] == jnp.arange(owners, dtype=jnp.int32)[None, :]).astype(f32)
    positive = jnp.sum(logits * target, 1)
    contrast_loss = (
        jnp.sum(-positive + 0.5 * jnp.log(row_total)) + 0.5 * jnp.sum(jnp.log(column_total))
    ) / owners
    grad_logits = (
        0.5 * expo / row_total[:, None] + 0.5 * expo / column_total[None, :] - target
    ) * (loss_scale / owners)
    grad_row = pick(grad_logits, owner_index, 0)
    grad_unit = jnp.sum(grad_row[:, None] * report_unit, 0) / contrast_divisor_factor
    grad_pooled = (grad_unit - pooled_unit * jnp.sum(pooled_unit * grad_unit)) * pooled_inverse
    grad_row_out = grad_pooled / count
    grad_low = grad_row_out.astype(bf16)

    up = contract(w_out, grad_low[None, :], 1, 1)
    up_heads = up.reshape(heads, HEAD, 1)
    pull = jnp.sum(up_heads * values, 1)
    pull_mean = jnp.sum(weights * pull[:, :, None], 1)
    grad_scores = (
        weights
        * (pull[:, :, None] - pull_mean[:, None, :])
        * (validity * (score_scale / HEAD))[None, None, :]
    ).astype(bf16)
    grad_query_unit = jnp.einsum("hdk,hkq->hdq", key_low, grad_scores, preferred_element_type=f32)
    grad_key_unit = jnp.einsum("hdq,hkq->hdk", query_low, grad_scores, preferred_element_type=f32)
    grad_q = query_scale * (
        grad_query_unit - query_unit * jnp.mean(query_unit * grad_query_unit, 1, keepdims=True)
    )
    grad_k = key_scale * (
        grad_key_unit - key_unit * jnp.mean(key_unit * grad_key_unit, 1, keepdims=True)
    )
    grad_v = up_heads * key_mass[:, None, :]
    grads_in = jnp.stack([grad_q, grad_k, grad_v]).astype(bf16).reshape(3 * heads * HEAD, length)
    grad_normed = jnp.dot(weights_in, grads_in, preferred_element_type=f32)
    first = jnp.mean(grad_normed, 0, keepdims=True)
    second = jnp.mean(grad_normed * normed, 0, keepdims=True)
    stats = jnp.concatenate([first, second], 0)
    stats_high = stats.astype(bf16)
    stats_low = (stats - stats_high.astype(f32)).astype(bf16)
    stats = jnp.concatenate([stats_high, stats_low, jnp.zeros((12, length), bf16)], 0)
    sending = jnp.concatenate(
        [
            grad_normed.astype(bf16).reshape(parts, block, length),
            jnp.broadcast_to(stats[None], (parts, 16, length)),
        ],
        1,
    )
    total = jnp.sum(exchange(sending, "mp").astype(f32), 0)
    first = total[block : block + 1] + total[block + 2 : block + 3]
    second = total[block + 1 : block + 2] + total[block + 3 : block + 4]
    own_normed = (chunk.astype(f32) - mean) * inverse
    own_grad = pick(grad_row_out.reshape(parts, block), part_index, 0)
    grad_rows = (
        own_grad[:, None] * validity[None, :]
        + (total[:block] - first - own_normed * second) * inverse
    ).astype(bf16)

    going = contract(select, grad_rows, 1, 1).astype(bf16)
    back = exchange(going.reshape(owners, ROWS, block), DP).reshape(owners * ROWS, block)
    grad_block = contract(back, dispatch, 0, 0).astype(bf16)
    grad_embedding = spread(grad_block, "mp", parts).reshape(width, tiles)

    def halves(values, axis):
        split = values.shape[:axis] + (chips, CORES, share) + values.shape[axis + 1 :]
        values = values.reshape(split)
        merged = split[:axis] + (chips * share,) + split[axis + 3 :]
        own = pick(values, core, axis + 1).reshape(merged)
        other = pick(values, 1 - core, axis + 1).reshape(merged)
        return own, other

    def reduce_over_owners(own, other):
        got = lax.ppermute(other.astype(bf16), "core", [(0, 1), (1, 0)])
        both = (own + got.astype(f32)).astype(bf16)
        return jnp.sum(exchange(both, "chip").astype(f32), 0)

    norm_own, norm_other = halves(slide_norm, 0)
    grads_wide = grads_in[: 2 * heads * HEAD]
    wide = (chips, share, 2 * heads * HEAD)
    grad_wide = reduce_over_owners(
        contract(norm_own, grads_wide, 1, 1).reshape(wide),
        contract(norm_other, grads_wide, 1, 1).reshape(wide),
    )
    grad_query = grad_wide[:, : heads * HEAD]
    grad_key = grad_wide[:, heads * HEAD :]
    value_rows = contract(key_mass.astype(bf16), slide_norm, 1, 1)
    pieces = jnp.concatenate(
        [
            value_rows.reshape(heads, owners, share).transpose(1, 0, 2).reshape(owners, -1),
            grad_row_out.astype(bf16).astype(f32).reshape(owners, share),
            jnp.broadcast_to(up.reshape(1, -1), (owners, heads * HEAD)),
            jnp.broadcast_to(attended_sum, (owners, heads * HEAD)),
        ],
        1,
    )
    pieces = jnp.pad(pieces, ((0, 0), (0, -pieces.shape[1] % 128)))
    pieces = exchange(pieces[:, None, :], DP)[:, 0, :]
    edge = heads * share
    from_values = pieces[:, :edge].reshape(owners, heads, share)
    from_grads = pieces[:, edge : edge + share]
    edge = edge + share
    from_up = pieces[:, edge : edge + heads * HEAD].reshape(owners, heads, HEAD)
    edge = edge + heads * HEAD
    from_attended = pieces[:, edge : edge + heads * HEAD]
    grad_value = jnp.einsum("ohs,ohd->shd", from_values, from_up, precision=exact)
    grad_value = grad_value.reshape(share, heads * HEAD)
    grad_out = contract(from_attended, from_grads, 0, 0, precision=exact)

    grad_hidden = (contract(grad_embedding, w_two, 0, 1) * gelu_slope(hidden_pre)).astype(bf16)
    tile_own, tile_other = halves(tile_norm, 1)
    grad_own, grad_other = halves(grad_embedding, 0)
    size = (chips, share, w_one.shape[1])

    def both_layers(tile_part, grad_part):
        one = contract(tile_part, grad_hidden, 0, 0).reshape(size)
        two = jnp.dot(grad_part, hidden, preferred_element_type=f32).reshape(size)
        return jnp.concatenate([one, two], 1)

    grad_tile = reduce_over_owners(
        both_layers(tile_own, grad_own), both_layers(tile_other, grad_other)
    )
    grad_one = grad_tile[:share]
    grad_two = grad_tile[share:].T
    return (contrast_loss, grad_one, grad_two, grad_query, grad_key, grad_value, grad_out)


def solution(mesh):
    owners, parts = mesh.devices.shape
    split = Mesh(
        mesh.devices.reshape(owners // CORES, CORES, parts), ("chip", "core", "mp")
    )
    return jax.shard_map(
        per_device,
        mesh=split,
        in_specs=(
            P(DP, None),
            P(DP, None),
            P(),
            P(DP, None),
            P(None, "mp"),
            P("mp", None),
            P(None, "mp"),
            P(None, "mp"),
            P(None, "mp"),
            P("mp", None),
        ),
        out_specs=(
            P(),
            P(DP, "mp"),
            P("mp", DP),
            P(DP, "mp"),
            P(DP, "mp"),
            P(DP, "mp"),
            P("mp", DP),
        ),
        check_vma=False,
    )
```

time: 881 us -> 351 us (0.40)
  waiting for transfers between devices: 683 us -> 146 us
  starting transfers between devices: 23 us -> 61.9 us
  blocking collectives: 49.1 us -> 12.3 us
  between operations: 17.2 us -> 4.56 us
    reduce_scatter x6 -> x0, waiting for transfers between devices: 472 us -> none  [the longest x1 89.1 us: per_device(): lax.psum_scatter(grad_two_local.astype(jnp.bfloat16), 'dp', scatter_dimen...]
    psum x3 -> x0, waiting for transfers between devices: 172 us -> none  [the longest x1 69.5 us: per_device(): embedding = (tile_float + lax.psum(partial_out, 'mp')).astype(jnp.bfloat16)]
    all_to_all x3 -> x11, waiting for transfers between devices: 38.7 us -> 146 us  [exchange(): return lax.all_to_all(values, axis, 0, 0, tiled=True)]
    all_gather x2 -> x0, blocking collectives: 49.1 us -> none  [the longest x1 24.6 us: per_device(): all_pooled = lax.all_gather(pooled[None, :], 'dp', axis=0, tiled=True)]
    all_to_all x3 -> x11, starting transfers between devices: 22.4 us -> 61.4 us  [exchange(): return lax.all_to_all(values, axis, 0, 0, tiled=True)]
    all_to_all x0 -> x1, blocking collectives: none -> 12.3 us  [exchange(): return lax.all_to_all(values, axis, 0, 0, tiled=True)]
    dot_general x25 -> x26, matrix products: 40.3 us -> 45.4 us  [the longest x14 21.8 us: contract(): lax.dot_general(left, right, (((left_dim,), (right_dim,)), ((), ())), pre...]
  transfers between devices with their start and end apart: 12 -> 13, of which waited for: 11 -> 11; matrix products, arithmetic and copies ran while one was open for 6% -> 14% of each run, Pallas kernels for 0% -> 0%
where the time goes in v1:
time: 351 us; the launch traced here: 348 us
  waiting for transfers between devices  146 us (42%)
  starting transfers between devices  61.9 us (18%)
  matrix products  48.5 us (14%)
  other arithmetic  38.5 us (11%)
  local copies, waits for them, and re-layouts  36.2 us (10%)
  blocking collectives  12.3 us (4%)
  between operations  4.56 us (1%)
    all_to_all x11, waiting for transfers between devices, exchange(): return lax.all_to_all(values, axis, 0, 0, tiled=True)  146 us
    all_to_all x11, starting transfers between devices, exchange(): return lax.all_to_all(values, axis, 0, 0, tiled=True)  61.4 us
    dot_general x14, matrix products, contract(): lax.dot_general(left, right, (((left_dim,), (right_dim,)), ((), ())), pre...  21.8 us
    unnamed x114, local copies, waits for them, and re-layouts  12.5 us
    all_to_all x1, blocking collectives, exchange(): return lax.all_to_all(values, axis, 0, 0, tiled=True)  12.3 us
  transfers between devices with their start and end apart: 13, of which 11 were waited for; matrix products, arithmetic and copies ran while one was open for 14% of the time, Pallas kernels for 0%

profile of v1, /device:TPU:8, one launch (start us, length us, event | category | flops | bytes accessed | tf_op | source)
XLA Modules:
  0.0 348.3 jit_solution(9364843901539911580)
XLA Ops:
  5.3 1.5 reshape.351
  6.8 2.2 copy.79
  9.0 8.6 %all-to-all-start.1 = ((bf16[8,192,192]{2,1,0:T(8,128)(2,1)}), bf16[8,192,192]{2,1,0:T(8,128)(2,1)S(1)}, u32[]{:S(2)}, u32[]{:S(2)}) async-start(bf16[8,192,192]{2,1,0:T(8,128)(2,1)} %bitcast.139), calls=%async_computation.1 | async-start | bytes 1572864 | tf_op jit(solution)/shard_map/all_to_all | solution.py:27
  17.6 2.4 reshape.350
  23.0 17.7 %all-to-all-done.1 = bf16[8,192,192]{2,1,0:T(8,128)(2,1)S(1)} async-done(((bf16[8,192,192]{2,1,0:T(8,128)(2,1)}), bf16[8,192,192]{2,1,0:T(8,128)(2,1)S(1)}, u32[]{:S(2)}, u32[]{:S(2)}) %all-to-all-start.1) | async-done | bytes 589856 | tf_op jit(solution)/shard_map/all_to_all | solution.py:27
  40.9 1.6 convolution_convert_fusion.4
  42.5 7.5 %all-to-all-start.2 = ((bf16[32,16,256]{2,1,0:T(8,128)(2,1)}), bf16[32,16,256]{2,1,0:T(8,128)(2,1)S(1)}, u32[]{:S(2)}, u32[]{:S(2)}) async-start(bf16[32,16,256]{2,1,0:T(8,128)(2,1)} %bitcast.3), calls=%async_computation.2 | async-start | bytes 524288 | tf_op jit(solution)/shard_map/all_to_all | solution.py:27
  52.6 4.9 %all-to-all-done.2 = bf16[32,16,256]{2,1,0:T(8,128)(2,1)S(1)} async-done(((bf16[32,16,256]{2,1,0:T(8,128)(2,1)}), bf16[32,16,256]{2,1,0:T(8,128)(2,1)S(1)}, u32[]{:S(2)}, u32[]{:S(2)}) %all-to-all-start.2) | async-done | bytes 262176 | tf_op jit(solution)/shard_map/all_to_all | solution.py:27
  57.5 5.2 %all-to-all-start = ((bf16[32,2,768]{2,1,0:T(2,128)(2,1)}), bf16[32,2,768]{2,1,0:T(2,128)(2,1)S(1)}, u32[]{:S(2)}, u32[]{:S(2)}) async-start(bf16[32,2,768]{2,1,0:T(2,128)(2,1)} %reshape.401), calls=%async_computation | async-start | bytes 196608 | tf_op jit(solution)/shard_map/all_to_all | solution.py:27
  64.4 4.8 %all-to-all-done = bf16[32,2,768]{2,1,0:T(2,128)(2,1)S(1)} async-done(((bf16[32,2,768]{2,1,0:T(2,128)(2,1)}), bf16[32,2,768]{2,1,0:T(2,128)(2,1)S(1)}, u32[]{:S(2)}, u32[]{:S(2)}) %all-to-all-start) | async-done | bytes 98336 | tf_op jit(solution)/shard_map/all_to_all | solution.py:27
  69.8 3.6 %all-to-all-start.3 = ((bf16[8,192,384]{2,1,0:T(8,128)(2,1)}), bf16[8,192,384]{2,1,0:T(8,128)(2,1)S(1)}, u32[]{:S(2)}, u32[]{:S(2)}) async-start(bf16[8,192,384]{2,1,0:T(8,128)(2,1)} %broadcast_in_dim.32), calls=%async_computation.3 | async-start | bytes 2359296 | tf_op jit(solution)/shard_map/all_to_all | solution.py:27
  74.7 1.9 constant_dynamic-update-slice_fusion.2
  78.3 1.6 reshape.402
  83.7 21.8 %all-to-all-done.3 = bf16[8,192,384]{2,1,0:T(8,128)(2,1)S(1)} async-done(((bf16[8,192,384]{2,1,0:T(8,128)(2,1)}), bf16[8,192,384]{2,1,0:T(8,128)(2,1)S(1)}, u32[]{:S(2)}, u32[]{:S(2)}) %all-to-all-start.3) | async-done | bytes 1179680 | tf_op jit(solution)/shard_map/all_to_all | solution.py:27
  106.1 2.6 fusion.16
  112.4 2.7 convolution_convert_fusion.6
  118.8 4.0 %all-to-all-start.4 = ((f32[8,1,1536]{2,1,0:T(1,128)}), f32[8,1,1536]{2,1,0:T(1,128)}, u32[]{:S(2)}, u32[]{:S(2)}) async-start(f32[8,1,1536]{2,1,0:T(1,128)} %broadcast_in_dim.33), calls=%async_computation.4 | async-start | bytes 98304 | tf_op jit(solution)/shard_map/all_to_all | solution.py:27
  123.9 7.1 %all-to-all-done.4 = f32[8,1,1536]{2,1,0:T(1,128)} async-done(((f32[8,1,1536]{2,1,0:T(1,128)}), f32[8,1,1536]{2,1,0:T(1,128)}, u32[]{:S(2)}, u32[]{:S(2)}) %all-to-all-start.4) | async-done | bytes 49184 | tf_op jit(solution)/shard_map/all_to_all | solution.py:27
  136.9 5.5 %all-to-all-start.5 = ((f32[32,1,128]{2,1,0:T(1,128)}), f32[32,1,128]{2,1,0:T(1,128)}, u32[]{:S(2)}, u32[]{:S(2)}) async-start(f32[32,1,128]{2,1,0:T(1,128)} %broadcast_in_dim.34), calls=%async_computation.5 | async-start | bytes 32768 | tf_op jit(solution)/shard_map/all_to_all | solution.py:27
  142.4 3.1 multiply_reduce_fusion.2
  145.6 2.9 all-to-all-done.5
  153.5 1.9 fusion.133
  156.8 1.7 multiply_reduce_fusion.6
  158.5 3.5 %multiply_reduce_fusion.5 = (f32[2,384]{1,0:T(2,128)}, f32[2,96,384]{2,1,0:T(8,128)}) fusion(f32[2,96,384]{2,1,0:T(8,128)} %bitcast.150, f32[2,384]{1,0:T(2,128)S(1)} %copy-done.29, bf16[2,96,384]{2,1,0:T(8,128)(2,1)} %copy-done.19, f32[2,384,384]{2,1,0:T(8,128)} %get-tuple-element.28, f32[384]{0:T(512)} %broadcast_multiply_fusion.4, ...), kind=kOutput, calls=%fused_computation.105 | convolution fusion | flops 58319232 | bytes 1927680 | tf_op jit(solution)/shard_map/hdk,hkq->hdq/dot_general | solution.py:168
  162.0 3.5 %multiply_reduce_fusion.4 = (f32[2,384]{1,0:T(2,128)}, f32[2,96,384]{2,1,0:T(8,128)}) fusion(f32[2,96,384]{2,1,0:T(8,128)} %bitcast.154, f32[2,384]{1,0:T(2,128)} %copy-done.30, bf16[2,96,384]{2,1,0:T(8,128)(2,1)} %copy-done.18, f32[2,384,384]{2,1,0:T(8,128)} %get-tuple-element.28, f32[384]{0:T(512)} %broadcast_multiply_fusion.4, ...), kind=kOutput, calls=%fused_computation.103 | convolution fusion | flops 58319232 | bytes 1927680 | tf_op jit(solution)/shard_map/hdq,hkq->hdk/dot_general | solution.py:169
  170.1 3.1 fusion.132
  174.6 4.4 %all-to-all-start.6 = ((bf16[8,208,384]{2,1,0:T(8,128)(2,1)}), bf16[8,208,384]{2,1,0:T(8,128)(2,1)}, u32[]{:S(2)}, u32[]{:S(2)}) async-start(bf16[8,208,384]{2,1,0:T(8,128)(2,1)} %pad_maximum_fusion.1), calls=%async_computation.6 | async-start | bytes 2555904 | tf_op jit(solution)/shard_map/all_to_all | solution.py:27
  181.6 31.6 %all-to-all-done.6 = bf16[8,208,384]{2,1,0:T(8,128)(2,1)} async-done(((bf16[8,208,384]{2,1,0:T(8,128)(2,1)}), bf16[8,208,384]{2,1,0:T(8,128)(2,1)}, u32[]{:S(2)}, u32[]{:S(2)}) %all-to-all-start.6) | async-done | bytes 1277984 | tf_op jit(solution)/shard_map/all_to_all | solution.py:27
  213.2 1.5 convert_reduce_fusion.1
  214.8 1.8 convolution_convert_fusion.5
  216.6 1.8 copy.51
  218.3 12.3 %all_to_all.60 = bf16[32,16,192]{2,1,0:T(8,128)(2,1)S(1)} all-to-all(bf16[32,16,192]{2,1,0:T(8,128)(2,1)} %bitcast.162), channel_id=1, replica_groups=mesh['chip'=16,'core'=2,'mp'=8] {'chip','core'}, dimensions={0} | all-to-all | bytes 393216 | tf_op jit(solution)/shard_map/all_to_all | solution.py:27
  232.6 4.2 %all-to-all-start.8 = ((bf16[8,192,192]{2,1,0:T(8,128)(2,1)}), bf16[8,192,192]{2,1,0:T(8,128)(2,1)}, u32[]{:S(2)}, u32[]{:S(2)}) async-start(bf16[8,192,192]{2,1,0:T(8,128)(2,1)} %broadcast_in_dim.37), calls=%async_computation.8 | async-start | bytes 1572864 | tf_op jit(solution)/shard_map/all_to_all | solution.py:27
  236.8 24.1 %all-to-all-done.8 = bf16[8,192,192]{2,1,0:T(8,128)(2,1)} async-done(((bf16[8,192,192]{2,1,0:T(8,128)(2,1)}), bf16[8,192,192]{2,1,0:T(8,128)(2,1)}, u32[]{:S(2)}, u32[]{:S(2)}) %all-to-all-start.8) | async-done | bytes 589856 | tf_op jit(solution)/shard_map/all_to_all | solution.py:27
  260.9 2.3 fusion.23
  263.3 1.6 convolution_convert_fusion.1
  265.4 1.6 pad_maximum_fusion
  271.4 3.1 fusion.24
  277.7 5.0 %all-to-all-start.11 = ((f32[32,1,640]{2,1,0:T(1,128)}), f32[32,1,640]{2,1,0:T(1,128)S(1)}, u32[]{:S(2)}, u32[]{:S(2)}) async-start(f32[32,1,640]{2,1,0:T(1,128)} %broadcast_in_dim.40), calls=%async_computation.11 | async-start | bytes 163840 | tf_op jit(solution)/shard_map/all_to_all | solution.py:27
  282.7 2.7 add_convert_fusion
  285.4 3.0 fusion.57
  289.1 6.6 %all-to-all-start.10 = ((bf16[16,48,384]{2,1,0:T(8,128)(2,1)}), bf16[16,48,384]{2,1,0:T(8,128)(2,1)S(1)}, u32[]{:S(2)}, u32[]{:S(2)}) async-start(bf16[16,48,384]{2,1,0:T(8,128)(2,1)} %add_convert_fusion), calls=%async_computation.10 | async-start | bytes 1179648 | tf_op jit(solution)/shard_map/all_to_all | solution.py:27
  295.7 1.6 fusion.54
  297.5 3.8 %fusion.1 = bf16[16,96,768]{2,1,0:T(8,128)(2,1)} fusion(f32[16,48,768]{2,1,0:T(8,128)S(1)} %copy-done.5, f32[16,48,768]{2,1,0:T(8,128)S(1)} %fusion.54, bf16[16,96,768]{2,1,0:T(8,128)(2,1)} %collective-permute-done), kind=kLoop, calls=%fused_computation.2 | loop fusion | flops 4718592 | bytes 9437184 | tf_op jit(solution)/shard_map/convert_element_type | solution.py:217
  301.3 4.4 %all-to-all-done.10 = bf16[16,48,384]{2,1,0:T(8,128)(2,1)S(1)} async-done(((bf16[16,48,384]{2,1,0:T(8,128)(2,1)}), bf16[16,48,384]{2,1,0:T(8,128)(2,1)S(1)}, u32[]{:S(2)}, u32[]{:S(2)}) %all-to-all-start.10) | async-done | bytes 589856 | tf_op jit(solution)/shard_map/all_to_all | solution.py:27
  305.6 6.9 %all-to-all-start.9 = ((bf16[16,96,768]{2,1,0:T(8,128)(2,1)}), bf16[16,96,768]{2,1,0:T(8,128)(2,1)}, u32[]{:S(2)}, u32[]{:S(2)}) async-start(bf16[16,96,768]{2,1,0:T(8,128)(2,1)} %fusion.1), calls=%async_computation.9 | async-start | bytes 4718592 | tf_op jit(solution)/shard_map/all_to_all | solution.py:27
  318.1 26.3 %all-to-all-done.9 = bf16[16,96,768]{2,1,0:T(8,128)(2,1)} async-done(((bf16[16,96,768]{2,1,0:T(8,128)(2,1)}), bf16[16,96,768]{2,1,0:T(8,128)(2,1)}, u32[]{:S(2)}, u32[]{:S(2)}) %all-to-all-start.9) | async-done | bytes 2359328 | tf_op jit(solution)/shard_map/all_to_all | solution.py:27
  344.4 2.0 convert_reduce_fusion
  (231 shorter events, 63.9 us)
Async XLA Ops:
  0.6 3.9 %copy-start = (bf16[768,1536]{1,0:T(8,128)(2,1)S(1)}, bf16[768,1536]{1,0:T(8,128)(2,1)}, u32[]{:S(2)}) copy-start(bf16[768,1536]{1,0:T(8,128)(2,1)} %param.15) | copy-start | bytes 7077892
  9.0 11.7 %copy-start.41 = (s32[192,1]{0,1:T(1,128)S(1)}, s32[192,1]{0,1:T(1,128)}, u32[]{:S(2)}) copy-start(s32[192,1]{0,1:T(1,128)} %param.11) | copy-start | bytes 2308
  9.0 31.7 %all-to-all-start.1 = ((bf16[8,192,192]{2,1,0:T(8,128)(2,1)}), bf16[8,192,192]{2,1,0:T(8,128)(2,1)S(1)}, u32[]{:S(2)}, u32[]{:S(2)}) async-start(bf16[8,192,192]{2,1,0:T(8,128)(2,1)} %bitcast.139), calls=%async_computation.1 | async-start | bytes 1572864 | tf_op jit(solution)/shard_map/all_to_all | solution.py:27
  20.0 30.0 %copy-start.42 = (bf16[1,1536]{1,0:T(2,128)(2,1)S(1)}, bf16[1,1536]{1,0:T(2,128)(2,1)}, u32[]{:S(2)}) copy-start(bf16[1,1536]{1,0:T(2,128)(2,1)} %param.13) | copy-start | bytes 9220
  23.0 29.6 %copy-start.48 = (s32[192]{0:T(256)}, s32[192]{0:T(256)S(1)}, u32[]{:S(2)}) copy-start(s32[192]{0:T(256)S(1)} %multiply_add_fusion) | copy-start | bytes 2308
  42.5 15.0 %all-to-all-start.2 = ((bf16[32,16,256]{2,1,0:T(8,128)(2,1)}), bf16[32,16,256]{2,1,0:T(8,128)(2,1)S(1)}, u32[]{:S(2)}, u32[]{:S(2)}) async-start(bf16[32,16,256]{2,1,0:T(8,128)(2,1)} %bitcast.3), calls=%async_computation.2 | async-start | bytes 524288 | tf_op jit(solution)/shard_map/all_to_all | solution.py:27
  52.6 16.6 %copy-start.47 = (s32[512]{0:T(512)}, s32[512]{0:T(512)S(1)}, u32[]{:S(2)}) copy-start(s32[512]{0:T(512)S(1)} %fusion.107) | copy-start | bytes 6148
  57.5 11.7 %all-to-all-start = ((bf16[32,2,768]{2,1,0:T(2,128)(2,1)}), bf16[32,2,768]{2,1,0:T(2,128)(2,1)S(1)}, u32[]{:S(2)}, u32[]{:S(2)}) async-start(bf16[32,2,768]{2,1,0:T(2,128)(2,1)} %reshape.401), calls=%async_computation | async-start | bytes 196608 | tf_op jit(solution)/shard_map/all_to_all | solution.py:27
  63.2 6.0 %copy-start.23 = (f32[256,384]{1,0:T(8,128)}, f32[256,384]{1,0:T(8,128)S(1)}, u32[]{:S(2)}) copy-start(f32[256,384]{1,0:T(8,128)S(1)} %fusion.32) | copy-start | bytes 1179652
  63.2 10.8 %copy-start.44 = (s32[32]{0:T(128)S(1)}, s32[32]{0:T(128)}, u32[]{:S(2)}) copy-start(s32[32]{0:T(128)} %param.12) | copy-start | bytes 388
  69.8 35.6 %all-to-all-start.3 = ((bf16[8,192,384]{2,1,0:T(8,128)(2,1)}), bf16[8,192,384]{2,1,0:T(8,128)(2,1)S(1)}, u32[]{:S(2)}, u32[]{:S(2)}) async-start(bf16[8,192,384]{2,1,0:T(8,128)(2,1)} %broadcast_in_dim.32), calls=%async_computation.3 | async-start | bytes 2359296 | tf_op jit(solution)/shard_map/all_to_all | solution.py:27
  74.0 2.6 copy-start.20
  74.0 3.4 copy-start.21
  81.1 2.0 copy-start.11
  83.1 27.3 %copy-start.35 = (f32[384]{0:T(512)}, f32[384]{0:T(512)S(1)}, u32[]{:S(2)}) copy-start(f32[384]{0:T(512)S(1)} %get-tuple-element.9) | copy-start | bytes 4612
  105.7 3.0 copy-start.26
  106.1 2.6 copy-start.32
  109.6 2.9 copy-start.30
  110.2 2.2 copy-start.28
  110.4 2.1 copy-start.19
  118.8 12.2 %all-to-all-start.4 = ((f32[8,1,1536]{2,1,0:T(1,128)}), f32[8,1,1536]{2,1,0:T(1,128)}, u32[]{:S(2)}, u32[]{:S(2)}) async-start(f32[8,1,1536]{2,1,0:T(1,128)} %broadcast_in_dim.33), calls=%async_computation.4 | async-start | bytes 98304 | tf_op jit(solution)/shard_map/all_to_all | solution.py:27
  136.9 11.5 %all-to-all-start.5 = ((f32[32,1,128]{2,1,0:T(1,128)}), f32[32,1,128]{2,1,0:T(1,128)}, u32[]{:S(2)}, u32[]{:S(2)}) async-start(f32[32,1,128]{2,1,0:T(1,128)} %broadcast_in_dim.34), calls=%async_computation.5 | async-start | bytes 32768 | tf_op jit(solution)/shard_map/all_to_all | solution.py:27
  142.4 9.5 %copy-start.43 = (f32[32]{0:T(128)S(1)}, f32[32]{0:T(128)}, u32[]{:S(2)}) copy-start(f32[32]{0:T(128)} %add_rsqrt_fusion.4) | copy-start | bytes 388
  142.4 16.1 %copy-start.29 = (f32[2,384]{1,0:T(2,128)S(1)}, f32[2,384]{1,0:T(2,128)}, u32[]{:S(2)}) copy-start(f32[2,384]{1,0:T(2,128)} %copy-done.28) | copy-start | bytes 9220
  150.0 5.5 %copy-start.45 = (f32[32]{0:T(128)}, f32[32]{0:T(128)S(1)}, u32[]{:S(2)}) copy-start(f32[32]{0:T(128)S(1)} %get-tuple-element.13) | copy-start | bytes 388
  156.8 5.2 %copy-start.38 = (f32[2,96]{1,0:T(2,128)}, f32[2,96]{1,0:T(2,128)S(1)}, u32[]{:S(2)}) copy-start(f32[2,96]{1,0:T(2,128)S(1)} %mul.417) | copy-start | bytes 2308
  158.5 9.2 %copy-start.31 = (f32[2,384]{1,0:T(2,128)S(1)}, f32[2,384]{1,0:T(2,128)}, u32[]{:S(2)}) copy-start(f32[2,384]{1,0:T(2,128)} %copy-done.30) | copy-start | bytes 9220
  165.6 4.4 %copy-start.27 = (f32[384]{0:T(512)S(1)}, f32[384]{0:T(512)}, u32[]{:S(2)}) copy-start(f32[384]{0:T(512)} %copy-done.26) | copy-start | bytes 4612
  165.6 4.5 %copy-start.33 = (f32[384]{0:T(512)S(1)}, f32[384]{0:T(512)}, u32[]{:S(2)}) copy-start(f32[384]{0:T(512)} %copy-done.32) | copy-start | bytes 4612
  170.0 3.2 copy-start.14
  170.1 3.2 copy-start.53
  174.6 40.2 %copy-start.34 = (f32[384]{0:T(512)S(1)}, f32[384]{0:T(512)}, u32[]{:S(2)}) copy-start(f32[384]{0:T(512)} %copy-done.32) | copy-start | bytes 4612
  174.6 40.2 %copy-start.36 = (f32[384]{0:T(512)S(1)}, f32[384]{0:T(512)}, u32[]{:S(2)}) copy-start(f32[384]{0:T(512)} %copy-done.35) | copy-start | bytes 4612
  174.6 38.6 %all-to-all-start.6 = ((bf16[8,208,384]{2,1,0:T(8,128)(2,1)}), bf16[8,208,384]{2,1,0:T(8,128)(2,1)}, u32[]{:S(2)}, u32[]{:S(2)}) async-start(bf16[8,208,384]{2,1,0:T(8,128)(2,1)} %pad_maximum_fusion.1), calls=%async_computation.6 | async-start | bytes 2555904 | tf_op jit(solution)/shard_map/all_to_all | solution.py:27
  232.6 28.3 %all-to-all-start.8 = ((bf16[8,192,192]{2,1,0:T(8,128)(2,1)}), bf16[8,192,192]{2,1,0:T(8,128)(2,1)}, u32[]{:S(2)}, u32[]{:S(2)}) async-start(bf16[8,192,192]{2,1,0:T(8,128)(2,1)} %broadcast_in_dim.37), calls=%async_computation.8 | async-start | bytes 1572864 | tf_op jit(solution)/shard_map/all_to_all | solution.py:27
  260.9 2.4 copy-start.3
  267.1 30.3 %collective-permute-start = (bf16[16,96,768]{2,1,0:T(8,128)(2,1)}, bf16[16,96,768]{2,1,0:T(8,128)(2,1)}, u32[]{:S(2)}, u32[]{:S(2)}) collective-permute-start(bf16[16,96,768]{2,1,0:T(8,128)(2,1)} %pad_maximum_fusion), channel_id=1, source_target_pairs={{0,8},{8,0},{1,9},{9,1},{2,10},{10,2},{3,11},{11,3},{4,12},{12,4},... | collective-permute-start | bytes 7077896 | tf_op jit(solution)/shard_map/ppermute | solution.py:216
  268.7 2.6 copy-start.10
  268.7 2.6 copy-start.37
  270.9 11.7 %collective-permute-start.1 = (bf16[16,48,384]{2,1,0:T(8,128)(2,1)}, bf16[16,48,384]{2,1,0:T(8,128)(2,1)}, u32[]{:S(2)}, u32[]{:S(2)}) collective-permute-start(bf16[16,48,384]{2,1,0:T(8,128)(2,1)} %convolution_convert_fusion.3), channel_id=1, source_target_pairs={{0,8},{8,0},{1,9},{9,1},{2,10},{10,2},{3,11},{11,3},{4,12},{12,4},... | collective-permute-start | bytes 1769480 | tf_op jit(solution)/shard_map/ppermute | solution.py:216
  274.5 10.9 %copy-start.4 = (f32[192,768]{1,0:T(8,128)S(1)}, f32[192,768]{1,0:T(8,128)}, u32[]{:S(2)}) copy-start(f32[192,768]{1,0:T(8,128)} %copy-done.2) | copy-start | bytes 1769476
  277.7 11.4 %all-to-all-start.11 = ((f32[32,1,640]{2,1,0:T(1,128)}), f32[32,1,640]{2,1,0:T(1,128)S(1)}, u32[]{:S(2)}, u32[]{:S(2)}) async-start(f32[32,1,640]{2,1,0:T(1,128)} %broadcast_in_dim.40), calls=%async_computation.11 | async-start | bytes 163840 | tf_op jit(solution)/shard_map/all_to_all | solution.py:27
  285.4 10.3 %copy-start.17 = (bf16[192,768,1]{1,0,2:T(8,128)(2,1)S(1)}, bf16[192,768,1]{1,0,2:T(8,128)(2,1)}, u32[]{:S(2)}) copy-start(bf16[192,768,1]{1,0,2:T(8,128)(2,1)} %copy-done.16) | copy-start | bytes 884740
  289.1 16.6 %all-to-all-start.10 = ((bf16[16,48,384]{2,1,0:T(8,128)(2,1)}), bf16[16,48,384]{2,1,0:T(8,128)(2,1)S(1)}, u32[]{:S(2)}, u32[]{:S(2)}) async-start(bf16[16,48,384]{2,1,0:T(8,128)(2,1)} %add_convert_fusion), calls=%async_computation.10 | async-start | bytes 1179648 | tf_op jit(solution)/shard_map/all_to_all | solution.py:27
  301.3 11.3 %copy-start.46 = (f32[32]{0:T(128)S(1)}, f32[32]{0:T(128)}, u32[]{:S(2)}) copy-start(f32[32]{0:T(128)} %copy-done.45) | copy-start | bytes 388
  301.3 12.5 %copy-start.51 = (f32[32]{0:T(128)S(1)}, f32[32]{0:T(128)}, u32[]{:S(2)}) copy-start(f32[32]{0:T(128)} %copy-done.50) | copy-start | bytes 388
  301.3 12.5 %copy-start.52 = (f32[32]{0:T(128)S(1)}, f32[32]{0:T(128)}, u32[]{:S(2)}) copy-start(f32[32]{0:T(128)} %get-tuple-element.15) | copy-start | bytes 388
  305.6 38.8 %all-to-all-start.9 = ((bf16[16,96,768]{2,1,0:T(8,128)(2,1)}), bf16[16,96,768]{2,1,0:T(8,128)(2,1)}, u32[]{:S(2)}, u32[]{:S(2)}) async-start(bf16[16,96,768]{2,1,0:T(8,128)(2,1)} %fusion.1), calls=%async_computation.9 | async-start | bytes 4718592 | tf_op jit(solution)/shard_map/all_to_all | solution.py:27
  (19 other events, 23.2 us)
